TPU v7x, 128 devices: a whole 4x4x4 slice. The times are simulated.
128 devices in a mesh: ctx: 32 (over x, y, core), head: 4 (over z).
Axes of the slice: x: 4, y: 4, z: 4, core: 2. Of those that a mesh axis runs over, the one named last changes fastest.
Arguments:
- queries: bfloat16 [24576, 2048], P(('ctx', 'head')), may hold values from -9 to 9
- keys: bfloat16 [24576, 2048], P(('ctx', 'head')), may hold values from -9 to 9
- values: bfloat16 [24576, 2048], P(('ctx', 'head')), may hold values from -12 to 12
- grad_out: bfloat16 [24576, 2048], P(('ctx', 'head')), may hold values from -6 to 6
- pattern: int32 [192, 16], replicated, may hold values from -1 to 191, as said below
Outputs:
- attn_out: bfloat16 [24576, 2048], P(('ctx', 'head'))
- grad_query: bfloat16 [24576, 2048], P(('ctx', 'head'))
- grad_key: bfloat16 [24576, 2048], P(('ctx', 'head'))
- grad_value: bfloat16 [24576, 2048], P(('ctx', 'head'))
Inputs may be any that keep to these rules, and one draw needn't show every extreme that they name: `pattern`: row b: entries 0 to 3 are the blocks b - 3 to b in order, -1 where such a number is negative; the remaining entries are, ascending, some of the blocks c <= b - 4 whose remainder modulo 16 equals one phase shared by all rows (each row its own subset, always holding the smallest such block where one exists), followed by -1.
All inputs are finite; a program needn't handle non-finite values.
Results may differ from a plain program's by a relative error of at most 0.015.
Values may be sent and summed in bfloat16 or wider, within the bound.
A program may use at most 128 MiB of HBM per device.

v0:
```python
import math
import jax
import jax.numpy as jnp
from jax import lax
from jax.sharding import PartitionSpec as P

HEAD_DIM = 128
HEAD_DEV = 4
BLOCK = 128
LOCAL = 4
STRIDE = 16
TOK_DEV = 768


def shifted(value, axis, steps):
    count = lax.axis_size(axis)
    first, last = (max(0, -steps), min(count, count - steps))
    return lax.ppermute(value, axis, [(source, source + steps) for source in range(first, last)])


def per_device(queries, keys, values, grad_out, pattern):
    query_here, key_here, value_here, grad_here = (
        lax.all_to_all(queries, "head", split_axis=1, concat_axis=0, tiled=True),
        lax.all_to_all(keys, "head", split_axis=1, concat_axis=0, tiled=True),
        lax.all_to_all(values, "head", split_axis=1, concat_axis=0, tiled=True),
        lax.all_to_all(grad_out, "head", split_axis=1, concat_axis=0, tiled=True),
    )
    device = lax.axis_index("ctx")
    cycle_size = lax.axis_size("ctx")
    blocks_here = TOK_DEV // BLOCK
    block_total = pattern.shape[0]
    strided_count = block_total // STRIDE
    owned_count = (blocks_here + STRIDE - 1) // STRIDE
    features = HEAD_DEV * HEAD_DIM
    score_scale = 1.0 / math.sqrt(HEAD_DIM)
    edge_rows = (LOCAL - 1) * BLOCK
    stride_phase = pattern[block_total - 1, LOCAL] % STRIDE
    first_local = jnp.mod(stride_phase - device * blocks_here, STRIDE)
    own_local = first_local + STRIDE * jnp.arange(owned_count, dtype=jnp.int32)
    own_valid = own_local < blocks_here
    own_safe = jnp.where(own_valid, own_local, 0)
    key_blocks = key_here.reshape(blocks_here, BLOCK, features)
    value_blocks = value_here.reshape(blocks_here, BLOCK, features)
    offer_keys = jnp.where(own_valid[:, None, None], key_blocks[own_safe], 0)
    offer_values = jnp.where(own_valid[:, None, None], value_blocks[own_safe], 0)
    pool_ids = stride_phase + STRIDE * jnp.arange(strided_count, dtype=jnp.int32)
    pool_owner = pool_ids // blocks_here
    slot_within = (pool_ids - pool_owner * blocks_here) // STRIDE
    pool_slots = pool_owner * owned_count + slot_within
    all_keys, all_values = (
        lax.all_gather(
            offer_keys.reshape(owned_count * BLOCK, features), "ctx", axis=0, tiled=True
        ),
        lax.all_gather(
            offer_values.reshape(owned_count * BLOCK, features), "ctx", axis=0, tiled=True
        ),
    )
    pool_keys = all_keys.reshape(cycle_size * owned_count, BLOCK, features)[pool_slots]
    pool_values = all_values.reshape(cycle_size * owned_count, BLOCK, features)[pool_slots]
    before_keys, before_values = shifted(
        (key_here[TOK_DEV - edge_rows :], value_here[TOK_DEV - edge_rows :]), "ctx", 1
    )
    window_keys = jnp.concatenate([before_keys, key_here], 0).reshape(
        edge_rows + TOK_DEV, HEAD_DEV, HEAD_DIM
    )
    window_values = jnp.concatenate([before_values, value_here], 0).reshape(
        edge_rows + TOK_DEV, HEAD_DEV, HEAD_DIM
    )
    pool_keys3 = pool_keys.reshape(strided_count * BLOCK, HEAD_DEV, HEAD_DIM)
    pool_values3 = pool_values.reshape(strided_count * BLOCK, HEAD_DEV, HEAD_DIM)
    my_rows = lax.dynamic_slice_in_dim(pattern, device * blocks_here, blocks_here, 0)
    span_rows = LOCAL * BLOCK
    key_place = jnp.arange(span_rows)
    query_place = jnp.arange(BLOCK)
    last_start = (LOCAL - 1) * BLOCK
    causal = (key_place[None, :] < last_start) | (
        key_place[None, :] - last_start <= query_place[:, None]
    )

    def attend_block(totals, operands):
        key_ext, value_ext, key_pool, value_pool = totals
        block_index, query_block, grad_block, pattern_row = operands
        near_keys = lax.dynamic_slice_in_dim(window_keys, block_index * BLOCK, span_rows, 0)
        near_values = lax.dynamic_slice_in_dim(window_values, block_index * BLOCK, span_rows, 0)
        joined_keys = jnp.concatenate([near_keys, pool_keys3], 0)
        joined_values = jnp.concatenate([near_values, pool_values3], 0)
        near_allowed = jnp.repeat(pattern_row[:LOCAL] >= 0, BLOCK)
        far_allowed = jnp.repeat(
            jnp.any(pattern_row[LOCAL:][None, :] == pool_ids[:, None], axis=1), BLOCK
        )
        allowed = jnp.concatenate(
            [
                causal & near_allowed[None, :],
                jnp.broadcast_to(far_allowed[None, :], (BLOCK, strided_count * BLOCK)),
            ],
            1,
        )
        scores = (
            jnp.einsum("qhd,khd->hqk", query_block, joined_keys, preferred_element_type=jnp.float32)
            * score_scale
        )
        masked = jnp.where(allowed[None], scores, -jnp.inf)
        row_top = jnp.max(masked, axis=2, keepdims=True)
        exponent = jnp.exp(masked - row_top)
        weights_wide = exponent / jnp.sum(exponent, axis=2, keepdims=True)
        weights = weights_wide.astype(jnp.bfloat16)
        output_wide = jnp.einsum(
            "hqk,khd->qhd", weights, joined_values, preferred_element_type=jnp.float32
        )
        grad_weights = jnp.einsum(
            "qhd,khd->hqk", grad_block, joined_values, preferred_element_type=jnp.float32
        )
        row_delta = jnp.sum(grad_block.astype(jnp.float32) * output_wide, axis=2).T[:, :, None]
        grad_scores = (score_scale * weights_wide * (grad_weights - row_delta)).astype(jnp.bfloat16)
        grad_query = jnp.einsum(
            "hqk,khd->qhd", grad_scores, joined_keys, preferred_element_type=jnp.float32
        )
        key_terms = jnp.einsum(
            "hqk,qhd->khd", grad_scores, query_block, preferred_element_type=jnp.float32
        )
        value_terms = jnp.einsum(
            "hqk,qhd->khd", weights, grad_block, preferred_element_type=jnp.float32
        )
        start_row = block_index * BLOCK
        key_ext = lax.dynamic_update_slice_in_dim(
            key_ext,
            lax.dynamic_slice_in_dim(key_ext, start_row, span_rows, 0) + key_terms[:span_rows],
            start_row,
            0,
        )
        value_ext = lax.dynamic_update_slice_in_dim(
            value_ext,
            lax.dynamic_slice_in_dim(value_ext, start_row, span_rows, 0) + value_terms[:span_rows],
            start_row,
            0,
        )
        key_pool = key_pool + key_terms[span_rows:]
        value_pool = value_pool + value_terms[span_rows:]
        return (
            (key_ext, value_ext, key_pool, value_pool),
            (output_wide.astype(jnp.bfloat16), grad_query.astype(jnp.bfloat16)),
        )

    ext_zero = jnp.zeros((edge_rows + TOK_DEV, HEAD_DEV, HEAD_DIM), jnp.float32)
    pool_zero = jnp.zeros((strided_count * BLOCK, HEAD_DEV, HEAD_DIM), jnp.float32)
    operands = (
        jnp.arange(blocks_here, dtype=jnp.int32),
        query_here.reshape(blocks_here, BLOCK, HEAD_DEV, HEAD_DIM),
        grad_here.reshape(blocks_here, BLOCK, HEAD_DEV, HEAD_DIM),
        my_rows,
    )
    (key_ext, value_ext, key_pool, value_pool), (outputs, query_grads) = lax.scan(
        attend_block, (ext_zero, ext_zero, pool_zero, pool_zero), operands
    )
    key_ext = key_ext.reshape(edge_rows + TOK_DEV, features)
    value_ext = value_ext.reshape(edge_rows + TOK_DEV, features)
    back_keys, back_values = (
        shifted(key_ext[:edge_rows].astype(jnp.bfloat16), "ctx", -1).astype(jnp.float32),
        shifted(value_ext[:edge_rows].astype(jnp.bfloat16), "ctx", -1).astype(jnp.float32),
    )
    own_keys = key_ext[edge_rows:] + jnp.pad(back_keys, ((TOK_DEV - edge_rows, 0), (0, 0)))
    own_values = value_ext[edge_rows:] + jnp.pad(back_values, ((TOK_DEV - edge_rows, 0), (0, 0)))
    pool_key_grads = key_pool.reshape(strided_count, BLOCK, features)
    pool_value_grads = value_pool.reshape(strided_count, BLOCK, features)
    slot_keys = (
        jnp.zeros((cycle_size * owned_count, BLOCK, features), jnp.float32)
        .at[pool_slots]
        .set(pool_key_grads)
    )
    slot_values = (
        jnp.zeros((cycle_size * owned_count, BLOCK, features), jnp.float32)
        .at[pool_slots]
        .set(pool_value_grads)
    )
    mine_keys, mine_values = (
        lax.psum_scatter(
            slot_keys.reshape(cycle_size * owned_count * BLOCK, features).astype(jnp.bfloat16),
            "ctx",
            scatter_dimension=0,
            tiled=True,
        ).astype(jnp.float32),
        lax.psum_scatter(
            slot_values.reshape(cycle_size * owned_count * BLOCK, features).astype(jnp.bfloat16),
            "ctx",
            scatter_dimension=0,
            tiled=True,
        ).astype(jnp.float32),
    )
    mine_keys = mine_keys.reshape(owned_count, BLOCK, features)
    mine_values = mine_values.reshape(owned_count, BLOCK, features)
    own_keys = (
        own_keys.reshape(blocks_here, BLOCK, features)
        .at[own_safe]
        .add(jnp.where(own_valid[:, None, None], mine_keys, 0.0))
    )
    own_values = (
        own_values.reshape(blocks_here, BLOCK, features)
        .at[own_safe]
        .add(jnp.where(own_valid[:, None, None], mine_values, 0.0))
    )
    attn_local = outputs.reshape(TOK_DEV, features)
    query_local = query_grads.reshape(TOK_DEV, features)
    key_local = own_keys.reshape(TOK_DEV, features).astype(jnp.bfloat16)
    value_local = own_values.reshape(TOK_DEV, features).astype(jnp.bfloat16)
    attn_out, grad_query, grad_key, grad_value = (
        lax.all_to_all(attn_local, "head", split_axis=0, concat_axis=1, tiled=True),
        lax.all_to_all(query_local, "head", split_axis=0, concat_axis=1, tiled=True),
        lax.all_to_all(key_local, "head", split_axis=0, concat_axis=1, tiled=True),
        lax.all_to_all(value_local, "head", split_axis=0, concat_axis=1, tiled=True),
    )
    return (attn_out, grad_query, grad_key, grad_value)


def solution(mesh):
    placed = (
        P(("ctx", "head"), None),
        P(("ctx", "head"), None),
        P(("ctx", "head"), None),
        P(("ctx", "head"), None),
        P(),
    )
    return jax.shard_map(
        per_device,
        mesh=mesh,
        in_specs=placed,
        out_specs=(
            P(("ctx", "head"), None),
            P(("ctx", "head"), None),
            P(("ctx", "head"), None),
            P(("ctx", "head"), None),
        ),
        check_vma=False,
    )
```

profile of v0, /device:TPU:0, one launch (start us, length us, event | category | flops | bytes accessed | tf_op | source)
XLA Modules:
  0.0 579.7 jit_solution(18047088099131019259)
XLA Ops:
  9.3 5.4 all-to-all-start.1
  17.3 9.7 %all-to-all-done.1 = bf16[192,4,512]{2,0,1:T(8,128)(2,1)S(1)} async-done(((bf16[192,4,512]{2,0,1:T(8,128)(2,1)}), bf16[192,4,512]{2,0,1:T(8,128)(2,1)S(1)}, u32[]{:S(2)}, u32[]{:S(2)}) %all-to-all-start.1) | async-done | bytes 786464 | tf_op jit(solution)/shard_map/all_to_all | solution.py:24
  27.9 13.9 %all_to_all.134 = bf16[192,4,512]{2,0,1:T(8,128)(2,1)S(1)} all-to-all(bf16[192,4,512]{2,0,1:T(8,128)(2,1)S(1)} %bitcast.174), channel_id=1, replica_groups=mesh['ctx'=32,'head'=4] {'head'}, dimensions={1} | all-to-all | bytes 1572864 | tf_op jit(solution)/shard_map/all_to_all | solution.py:25
  43.4 3.5 all-to-all-start
  47.9 9.4 %all-to-all-done = bf16[192,4,512]{2,0,1:T(8,128)(2,1)S(1)} async-done(((bf16[192,4,512]{2,0,1:T(8,128)(2,1)}), bf16[192,4,512]{2,0,1:T(8,128)(2,1)S(1)}, u32[]{:S(2)}, u32[]{:S(2)}) %all-to-all-start) | async-done | bytes 786464 | tf_op jit(solution)/shard_map/all_to_all | solution.py:23
  57.4 3.5 all-to-all-start.2
  65.3 3.5 collective-permute-start.1
  75.1 4.9 pad_maximum_fusion
  80.0 5.7 pad_maximum_fusion.1
  85.8 4.0 gather_fusion
  93.6 27.4 %all-gather.7.cloned.1.call-done = bf16[1,4096,512]{2,1,0:T(8,128)(2,1)} async-done(((bf16[1,128,512]{2,1,0:T(8,128)(2,1)}), bf16[1,4096,512]{2,1,0:T(8,128)(2,1)}) %all-gather.7.cloned.1.call-update) | async-done | bytes 4194320 | tf_op jit(solution)/shard_map/all_gather | solution.py:54
  121.0 4.0 gather_fusion.1
  131.9 219.7 %while.25 = (s32[]{:T(128)}, f32[1152,4,128]{0,2,1:T(8,128)}, f32[1152,4,128]{0,2,1:T(8,128)}, f32[1536,4,128]{0,2,1:T(8,128)}, f32[1536,4,128]{0,2,1:T(8,128)},...) while((s32[]{:T(128)}, f32[1152,4,128]{0,2,1:T(8,128)}, ...), condition=%wide.region_5.6_spmd.clone, body=%wide.region_0.5_spmd.clone.sunk | while | flops 1626605312 | bytes 194795088 | solution.py:152
  141.6 3.4 fusion.54
  145.0 2.8 fusion.55
  159.6 3.5 fusion.56
  178.2 3.4 fusion.54
  181.6 2.8 fusion.55
  196.2 3.6 fusion.56
  214.8 3.4 fusion.54
  218.2 2.8 fusion.55
  232.8 3.6 fusion.56
  251.4 3.4 fusion.54
  254.9 2.8 fusion.55
  269.5 3.6 fusion.56
  288.1 3.4 fusion.54
  291.5 2.8 fusion.55
  306.1 3.6 fusion.56
  324.7 3.4 fusion.54
  342.7 3.6 fusion.56
  351.6 3.2 copy.143
  354.9 2.9 reshape.381
  357.7 4.3 broadcast.237.clone
  362.1 6.1 %scatter_fusion = f32[32,128,512]{2,1,0:T(8,128)} fusion(f32[32,128,512]{2,1,0:T(8,128)} %broadcast.237.clone, s32[12]{0:T(128)S(1)} %fusion.22, f32[12,128,512]{2,1,0:T(8,128)S(1)} %copy-done.11), kind=kCustom, calls=%fused_computation.2 | custom fusion | bytes 9437232 | tf_op jit(solution)/shard_map/scatter | solution.py:168
  368.2 6.0 %convert_element_type.67 = bf16[32,128,512]{2,1,0:T(8,128)(2,1)} convert(f32[32,128,512]{2,1,0:T(8,128)} %scatter_fusion) | non-fusion elementwise | flops 2097152 | bytes 12582912 | tf_op jit(solution)/shard_map/convert_element_type | solution.py:177
  376.1 2.8 copy.147
  378.9 3.3 reshape.389
  382.2 4.3 broadcast.237.clone.1
  386.6 6.3 %scatter_fusion.1 = f32[32,128,512]{2,1,0:T(8,128)} fusion(f32[32,128,512]{2,1,0:T(8,128)} %broadcast.237.clone.1, s32[12]{0:T(128)S(1)} %fusion.22, f32[12,128,512]{2,1,0:T(8,128)S(1)} %reshape.389), kind=kCustom, calls=%fused_computation.3 | custom fusion | bytes 9437232 | tf_op jit(solution)/shard_map/scatter | solution.py:173
  392.8 6.2 %convert_element_type.73 = bf16[32,128,512]{2,1,0:T(8,128)(2,1)} convert(f32[32,128,512]{2,1,0:T(8,128)} %scatter_fusion.1) | non-fusion elementwise | flops 2097152 | bytes 12582912 | tf_op jit(solution)/shard_map/convert_element_type | solution.py:183
  401.3 4.5 all-to-all-start.5
  422.8 4.7 all-to-all-start.4
  429.3 27.1 %reduce-scatter.3.cloned.1.call-done = bf16[128,512]{1,0:T(8,128)(2,1)} async-done(((bf16[4096,512]{1,0:T(8,128)(2,1)}), bf16[128,512]{1,0:T(8,128)(2,1)}) %reduce-scatter.3.cloned.1.call-update) | async-done | bytes 131088 | tf_op jit(solution)/shard_map/reduce_scatter | solution.py:176
  456.4 85.2 %reduce-scatter.5.cloned.1.call-done = bf16[128,512]{1,0:T(8,128)(2,1)} async-done(((bf16[4096,512]{1,0:T(8,128)(2,1)}), bf16[128,512]{1,0:T(8,128)(2,1)}) %reduce-scatter.5.cloned.1.call-update) | async-done | bytes 131088 | tf_op jit(solution)/shard_map/reduce_scatter | solution.py:182
  544.2 4.4 all-to-all-start.6
  549.6 9.7 %all-to-all-done.6 = bf16[4,192,512]{2,1,0:T(8,128)(2,1)S(1)} async-done(((bf16[4,192,512]{2,1,0:T(8,128)(2,1)}), bf16[4,192,512]{2,1,0:T(8,128)(2,1)S(1)}, u32[]{:S(2)}, u32[]{:S(2)}) %all-to-all-start.6) | async-done | bytes 786464 | tf_op jit(solution)/shard_map/all_to_all | solution.py:208
  559.3 3.5 all-to-all-start.7
  568.0 4.3 all-to-all-done.7
  (402 shorter events, 218.9 us)
Async XLA Ops:
  7.2 7.6 %copy-start.21 = (s32[192,16]{0,1:T(8,128)S(1)}, s32[192,16]{0,1:T(8,128)}, u32[]{:S(2)}) copy-start(s32[192,16]{0,1:T(8,128)} %param.15) | copy-start | bytes 36868
  7.2 20.6 %copy-start.16 = (bf16[192,2048]{1,0:T(8,128)(2,1)S(1)}, bf16[192,2048]{1,0:T(8,128)(2,1)}, u32[]{:S(2)}) copy-start(bf16[192,2048]{1,0:T(8,128)(2,1)} %param.13) | copy-start | bytes 2359300
  9.3 17.7 %all-to-all-start.1 = ((bf16[192,4,512]{2,0,1:T(8,128)(2,1)}), bf16[192,4,512]{2,0,1:T(8,128)(2,1)S(1)}, u32[]{:S(2)}, u32[]{:S(2)}) async-start(bf16[192,4,512]{2,0,1:T(8,128)(2,1)} %bitcast.108), calls=%async_computation.1 | async-start | bytes 1572864 | tf_op jit(solution)/shard_map/all_to_all | solution.py:24
  14.7 27.7 %copy-start.17 = (bf16[192,2048]{1,0:T(8,128)(2,1)S(1)}, bf16[192,2048]{1,0:T(8,128)(2,1)}, u32[]{:S(2)}) copy-start(bf16[192,2048]{1,0:T(8,128)(2,1)} %param.11) | copy-start | bytes 2359300
  14.7 71.0 %all-gather.5.cloned.1.call-start = ((), (), s32[]{:S(2)}) async-start(), calls=%async_computation.12 | async-start | bytes 4325376 | tf_op jit(solution)/shard_map/all_gather | solution.py:51
  27.7 93.3 %all-gather.7.cloned.1.call-start = ((), (), s32[]{:S(2)}) async-start(), calls=%async_computation.13 | async-start | bytes 4325376 | tf_op jit(solution)/shard_map/all_gather | solution.py:54
  27.8 19.1 %copy-start.18 = (bf16[192,2048]{1,0:T(8,128)(2,1)S(1)}, bf16[192,2048]{1,0:T(8,128)(2,1)}, u32[]{:S(2)}) copy-start(bf16[192,2048]{1,0:T(8,128)(2,1)} %param.14) | copy-start | bytes 2359300
  43.4 13.9 %all-to-all-start = ((bf16[192,4,512]{2,0,1:T(8,128)(2,1)}), bf16[192,4,512]{2,0,1:T(8,128)(2,1)S(1)}, u32[]{:S(2)}, u32[]{:S(2)}) async-start(bf16[192,4,512]{2,0,1:T(8,128)(2,1)} %bitcast.109), calls=%async_computation | async-start | bytes 1572864 | tf_op jit(solution)/shard_map/all_to_all | solution.py:23
  57.4 14.7 %all-to-all-start.2 = ((bf16[192,4,512]{2,0,1:T(8,128)(2,1)}), bf16[192,4,512]{2,0,1:T(8,128)(2,1)S(1)}, u32[]{:S(2)}, u32[]{:S(2)}) async-start(bf16[192,4,512]{2,0,1:T(8,128)(2,1)} %bitcast.107), calls=%async_computation.2 | async-start | bytes 1572864 | tf_op jit(solution)/shard_map/all_to_all | solution.py:26
  60.9 395.5 %reduce-scatter.3.cloned.1.call-start = ((), (), s32[]{:S(2)}) async-start(), calls=%async_computation.10 | async-start | bytes 4325376 | tf_op jit(solution)/shard_map/reduce_scatter | solution.py:176
  62.4 10.6 %collective-permute-start = (bf16[384,512]{1,0:T(8,128)(2,1)}, bf16[384,512]{1,0:T(8,128)(2,1)}, u32[]{:S(2)}, u32[]{:S(2)}) collective-permute-start(bf16[384,512]{1,0:T(8,128)(2,1)} %bitcast.2), channel_id=1, source_target_pairs={{0,4},{4,8},{8,12},{12,16},{16,20},{20,24},{24,28},{28,32},{32,36}... | collective-permute-start | bytes 1179656 | tf_op jit(solution)/shard_map/ppermute | solution.py:18
  65.3 9.4 %collective-permute-start.1 = (bf16[384,512]{1,0:T(8,128)(2,1)}, bf16[384,512]{1,0:T(8,128)(2,1)S(1)}, u32[]{:S(2)}, u32[]{:S(2)}) collective-permute-start(bf16[384,512]{1,0:T(8,128)(2,1)} %bitcast.13), channel_id=1, source_target_pairs={{0,4},{4,8},{8,12},{12,16},{16,20},{20,24},{24,28},{28,32},{32,36}... | collective-permute-start | bytes 1179656 | tf_op jit(solution)/shard_map/ppermute | solution.py:18
  74.4 5.6 copy-start.14
  131.9 5.9 %copy-start.12 = (bf16[1152,4,128]{2,1,0:T(4,128)(2,1)}, bf16[1152,4,128]{2,1,0:T(4,128)(2,1)S(1)}, u32[]{:S(2)}) copy-start(bf16[1152,4,128]{2,1,0:T(4,128)(2,1)S(1)} %get-tuple-element.535) | copy-start | bytes 3538948 | tf_op jit(solution)/shard_map/while
  133.2 4.9 copy-start.9
  138.3 6.7 %copy-start.7 = (bf16[2048,4,128]{2,0,1:T(8,128)(2,1)}, bf16[2048,4,128]{2,0,1:T(8,128)(2,1)S(1)}, u32[]{:S(2)}) copy-start(bf16[2048,4,128]{2,0,1:T(8,128)(2,1)S(1)} %constant_dynamic-update-slice_fusion.5) | copy-start | bytes 6291460 | tf_op jit(solution)/shard_map/while
  159.6 4.2 copy-start.4
  163.7 4.8 copy-start.13
  168.5 5.9 %copy-start.12 = (bf16[1152,4,128]{2,1,0:T(4,128)(2,1)}, bf16[1152,4,128]{2,1,0:T(4,128)(2,1)S(1)}, u32[]{:S(2)}) copy-start(bf16[1152,4,128]{2,1,0:T(4,128)(2,1)S(1)} %get-tuple-element.535) | copy-start | bytes 3538948 | tf_op jit(solution)/shard_map/while
  169.9 4.9 copy-start.9
  175.0 6.7 %copy-start.7 = (bf16[2048,4,128]{2,0,1:T(8,128)(2,1)}, bf16[2048,4,128]{2,0,1:T(8,128)(2,1)S(1)}, u32[]{:S(2)}) copy-start(bf16[2048,4,128]{2,0,1:T(8,128)(2,1)S(1)} %constant_dynamic-update-slice_fusion.5) | copy-start | bytes 6291460 | tf_op jit(solution)/shard_map/while
  196.2 4.2 copy-start.4
  200.4 4.8 copy-start.13
  205.1 5.9 %copy-start.12 = (bf16[1152,4,128]{2,1,0:T(4,128)(2,1)}, bf16[1152,4,128]{2,1,0:T(4,128)(2,1)S(1)}, u32[]{:S(2)}) copy-start(bf16[1152,4,128]{2,1,0:T(4,128)(2,1)S(1)} %get-tuple-element.535) | copy-start | bytes 3538948 | tf_op jit(solution)/shard_map/while
  206.5 4.9 copy-start.9
  211.6 6.7 %copy-start.7 = (bf16[2048,4,128]{2,0,1:T(8,128)(2,1)}, bf16[2048,4,128]{2,0,1:T(8,128)(2,1)S(1)}, u32[]{:S(2)}) copy-start(bf16[2048,4,128]{2,0,1:T(8,128)(2,1)S(1)} %constant_dynamic-update-slice_fusion.5) | copy-start | bytes 6291460 | tf_op jit(solution)/shard_map/while
  237.0 4.8 copy-start.13
  241.8 5.9 %copy-start.12 = (bf16[1152,4,128]{2,1,0:T(4,128)(2,1)}, bf16[1152,4,128]{2,1,0:T(4,128)(2,1)S(1)}, u32[]{:S(2)}) copy-start(bf16[1152,4,128]{2,1,0:T(4,128)(2,1)S(1)} %get-tuple-element.535) | copy-start | bytes 3538948 | tf_op jit(solution)/shard_map/while
  243.1 4.9 copy-start.9
  248.2 6.7 %copy-start.7 = (bf16[2048,4,128]{2,0,1:T(8,128)(2,1)}, bf16[2048,4,128]{2,0,1:T(8,128)(2,1)S(1)}, u32[]{:S(2)}) copy-start(bf16[2048,4,128]{2,0,1:T(8,128)(2,1)S(1)} %constant_dynamic-update-slice_fusion.5) | copy-start | bytes 6291460 | tf_op jit(solution)/shard_map/while
  273.6 4.8 copy-start.13
  278.4 5.9 %copy-start.12 = (bf16[1152,4,128]{2,1,0:T(4,128)(2,1)}, bf16[1152,4,128]{2,1,0:T(4,128)(2,1)S(1)}, u32[]{:S(2)}) copy-start(bf16[1152,4,128]{2,1,0:T(4,128)(2,1)S(1)} %get-tuple-element.535) | copy-start | bytes 3538948 | tf_op jit(solution)/shard_map/while
  279.7 4.9 copy-start.9
  284.8 6.7 %copy-start.7 = (bf16[2048,4,128]{2,0,1:T(8,128)(2,1)}, bf16[2048,4,128]{2,0,1:T(8,128)(2,1)S(1)}, u32[]{:S(2)}) copy-start(bf16[2048,4,128]{2,0,1:T(8,128)(2,1)S(1)} %constant_dynamic-update-slice_fusion.5) | copy-start | bytes 6291460 | tf_op jit(solution)/shard_map/while
  310.2 4.8 copy-start.13
  315.0 5.9 %copy-start.12 = (bf16[1152,4,128]{2,1,0:T(4,128)(2,1)}, bf16[1152,4,128]{2,1,0:T(4,128)(2,1)S(1)}, u32[]{:S(2)}) copy-start(bf16[1152,4,128]{2,1,0:T(4,128)(2,1)S(1)} %get-tuple-element.535) | copy-start | bytes 3538948 | tf_op jit(solution)/shard_map/while
  316.3 4.9 copy-start.9
  321.4 6.7 %copy-start.7 = (bf16[2048,4,128]{2,0,1:T(8,128)(2,1)}, bf16[2048,4,128]{2,0,1:T(8,128)(2,1)S(1)}, u32[]{:S(2)}) copy-start(bf16[2048,4,128]{2,0,1:T(8,128)(2,1)S(1)} %constant_dynamic-update-slice_fusion.5) | copy-start | bytes 6291460 | tf_op jit(solution)/shard_map/while
  346.9 4.8 copy-start.13
  357.7 4.3 copy-start.11
  374.3 167.3 %reduce-scatter.5.cloned.1.call-start = ((), (), s32[]{:S(2)}) async-start(), calls=%async_computation.11 | async-start | bytes 4325376 | tf_op jit(solution)/shard_map/reduce_scatter | solution.py:182
  401.3 11.4 %copy-start.22 = (s32[3]{0:T(128)S(1)}, s32[3]{0:T(128)}, u32[]{:S(2)}) copy-start(s32[3]{0:T(128)} %constant.137.clone.1) | copy-start | bytes 40
  401.3 21.4 %all-to-all-start.5 = ((bf16[4,192,512]{2,1,0:T(8,128)(2,1)}), bf16[4,192,512]{2,1,0:T(8,128)(2,1)}, u32[]{:S(2)}, u32[]{:S(2)}) async-start(bf16[4,192,512]{2,1,0:T(8,128)(2,1)} %all_to_all.116), calls=%async_computation.5 | async-start | bytes 1572864 | tf_op jit(solution)/shard_map/all_to_all | solution.py:207
  408.0 19.5 %collective-permute-start.3 = (bf16[384,512]{1,0:T(8,128)(2,1)}, bf16[384,512]{1,0:T(8,128)(2,1)S(1)}, u32[]{:S(2)}, u32[]{:S(2)}) collective-permute-start(bf16[384,512]{1,0:T(8,128)(2,1)} %copy.157), channel_id=1, source_target_pairs={{4,0},{8,4},{12,8},{16,12},{20,16},{24,20},{28,24},{32,28},{36,32}... | collective-permute-start | bytes 1179656 | tf_op jit(solution)/shard_map/ppermute | solution.py:18
  411.4 16.2 %collective-permute-start.2 = (bf16[384,512]{1,0:T(8,128)(2,1)}, bf16[384,512]{1,0:T(8,128)(2,1)}, u32[]{:S(2)}, u32[]{:S(2)}) collective-permute-start(bf16[384,512]{1,0:T(8,128)(2,1)} %copy.155), channel_id=1, source_target_pairs={{4,0},{8,4},{12,8},{16,12},{20,16},{24,20},{28,24},{32,28},{36,32}... | collective-permute-start | bytes 1179656 | tf_op jit(solution)/shard_map/ppermute | solution.py:18
  422.8 121.4 %all-to-all-start.4 = ((bf16[4,192,512]{2,1,0:T(8,128)(2,1)}), bf16[4,192,512]{2,1,0:T(8,128)(2,1)}, u32[]{:S(2)}, u32[]{:S(2)}) async-start(bf16[4,192,512]{2,1,0:T(8,128)(2,1)} %all_to_all.112), calls=%async_computation.4 | async-start | bytes 1572864 | tf_op jit(solution)/shard_map/all_to_all | solution.py:206
  544.2 15.1 %all-to-all-start.6 = ((bf16[4,192,512]{2,1,0:T(8,128)(2,1)}), bf16[4,192,512]{2,1,0:T(8,128)(2,1)S(1)}, u32[]{:S(2)}, u32[]{:S(2)}) async-start(bf16[4,192,512]{2,1,0:T(8,128)(2,1)} %bitcast.175), calls=%async_computation.7 | async-start | bytes 1572864 | tf_op jit(solution)/shard_map/all_to_all | solution.py:208
  559.3 13.0 %all-to-all-start.7 = ((bf16[4,192,512]{2,1,0:T(8,128)(2,1)}), bf16[4,192,512]{2,1,0:T(8,128)(2,1)S(1)}, u32[]{:S(2)}, u32[]{:S(2)}) async-start(bf16[4,192,512]{2,1,0:T(8,128)(2,1)} %bitcast.31), calls=%async_computation.9 | async-start | bytes 1572864 | tf_op jit(solution)/shard_map/all_to_all | solution.py:209
  (50 other events, 132.3 us)
Sparse Core Ops, SparseCore 0:
  27.8 45.4 all-gather.4
  75.6 45.3 all-gather.6
  374.4 81.9 reduce-scatter.2
  460.3 81.1 reduce-scatter.4
where the time goes:
time: 583 us; the launch traced here: 580 us
  local copies, waits for them, and re-layouts  176 us (30%)
  waiting for transfers between devices  173 us (30%)
  other arithmetic  83.8 us (14%)
  matrix products  74.7 us (13%)
  starting transfers between devices  37.7 us (6%)
  between operations  16.1 us (3%)
  blocking collectives  13.9 us (2%)
    reduce_scatter x1, waiting for transfers between devices, per_device(): lax.psum_scatter(slot_values.reshape(cycle_size * owned_count * BLOCK, fe...  85.2 us
    while x156, local copies, waits for them, and re-layouts  40.2 us
    all_gather x1, waiting for transfers between devices, per_device(): lax.all_gather(offer_values.reshape(owned_count * BLOCK, features), 'ctx'...  27.4 us
    reduce_scatter x1, waiting for transfers between devices, per_device(): lax.psum_scatter(slot_keys.reshape(cycle_size * owned_count * BLOCK, feat...  27.1 us
    dynamic_update_slice x6, other arithmetic, attend_block(): lax.dynamic_update_slice_in_dim(value_ext, lax.dynamic_slice_in_dim(value...  21.6 us
    sub x6, matrix products, attend_block(): exponent = jnp.exp(masked - row_top)  20.4 us
    dynamic_slice x24, local copies, waits for them, and re-layouts, per_device(): lax.scan(attend_block, (ext_zero, ext_zero, pool_zero, pool_zero), operands)  20.3 us
    convert_element_type x6, other arithmetic, attend_block(): weights = weights_wide.astype(jnp.bfloat16)  16.7 us
  transfers between devices with their start and end apart: 15, of which 7 were waited for; matrix products, arithmetic and copies ran while one was open for 13% of the time, Pallas kernels for 0%

commit v1 on v0

--- a/solution.py
+++ b/solution.py
@@ -10,6 +10,14 @@
 LOCAL = 4
 STRIDE = 16
 TOK_DEV = 768
+
+
+def _test_classes(page, array_axis):
+    z_new = lax.axis_size("ctx")
+    row_out = jnp.stack([page] * z_new)
+    shaped = lax.all_to_all(row_out, "ctx", split_axis=0, concat_axis=0)
+    state_next = jnp.concatenate(shaped, array_axis)
+    return state_next
 
 
 def shifted(value, axis, steps):
@@ -51,9 +59,7 @@
         lax.all_gather(
             offer_keys.reshape(owned_count * BLOCK, features), "ctx", axis=0, tiled=True
         ),
-        lax.all_gather(
-            offer_values.reshape(owned_count * BLOCK, features), "ctx", axis=0, tiled=True
-        ),
+        _test_classes(offer_values.reshape(owned_count * BLOCK, features), 0),
     )
     pool_keys = all_keys.reshape(cycle_size * owned_count, BLOCK, features)[pool_slots]
     pool_values = all_values.reshape(cycle_size * owned_count, BLOCK, features)[pool_slots]

time: 583 us -> 618 us (1.060)
  waiting for transfers between devices: 173 us -> 207 us
  blocking collectives: 13.9 us -> 0 us
  starting transfers between devices: 37.7 us -> 48.8 us
    all_to_all x0 -> x2, waiting for transfers between devices: none -> 35.7 us  [the longest x1 27.7 us: _test_classes(): shaped = lax.all_to_all(row_out, 'ctx', split_axis=0, concat_axis=0)]
    all_gather x1 -> x0, waiting for transfers between devices: 27.4 us -> none  [per_device(): lax.all_gather(offer_values.reshape(owned_count * BLOCK, features), 'ctx'...]
    all_to_all x1 -> x0, blocking collectives: 13.9 us -> none  [per_device(): lax.all_to_all(values, 'head', split_axis=1, concat_axis=0, tiled=True)]
    reduce_scatter x1, waiting for transfers between devices: 27.1 us -> 39.6 us  [per_device(): lax.psum_scatter(slot_keys.reshape(cycle_size * owned_count * BLOCK, feat...]
    all_to_all x0 -> x2, starting transfers between devices: none -> 11 us  [the longest x1 7.46 us: _test_classes(): shaped = lax.all_to_all(row_out, 'ctx', split_axis=0, concat_axis=0)]
    all_to_all x1, waiting for transfers between devices: 0.01 us -> 9.43 us  [per_device(): lax.all_to_all(grad_out, 'head', split_axis=1, concat_axis=0, tiled=True)]
  transfers between devices with their start and end apart: 15 -> 16, of which waited for: 7 -> 10; matrix products, arithmetic and copies ran while one was open for 13% -> 13% of each run, Pallas kernels for 0% -> 0%
where the time goes in v1:
time: 618 us; the launch traced here: 615 us
  waiting for transfers between devices  207 us (33%)
  local copies, waits for them, and re-layouts  180 us (29%)
  other arithmetic  82.9 us (13%)
  matrix products  74.7 us (12%)
  starting transfers between devices  48.8 us (8%)
  between operations  16.1 us (3%)
    reduce_scatter x1, waiting for transfers between devices, per_device(): lax.psum_scatter(slot_values.reshape(cycle_size * owned_count * BLOCK, fe...  85.3 us
    while x156, local copies, waits for them, and re-layouts  40.1 us
    reduce_scatter x1, waiting for transfers between devices, per_device(): lax.psum_scatter(slot_keys.reshape(cycle_size * owned_count * BLOCK, feat...  39.6 us
    all_to_all x1, waiting for transfers between devices, _test_classes(): shaped = lax.all_to_all(row_out, 'ctx', split_axis=0, concat_axis=0)  27.7 us
    dynamic_update_slice x6, other arithmetic, attend_block(): lax.dynamic_update_slice_in_dim(value_ext, lax.dynamic_slice_in_dim(value...  21.4 us
    sub x6, matrix products, attend_block(): exponent = jnp.exp(masked - row_top)  20.4 us
    dynamic_slice x24, local copies, waits for them, and re-layouts, per_device(): lax.scan(attend_block, (ext_zero, ext_zero, pool_zero, pool_zero), operands)  20.3 us
    convert_element_type x6, other arithmetic, attend_block(): weights = weights_wide.astype(jnp.bfloat16)  16.7 us
  transfers between devices with their start and end apart: 16, of which 10 were waited for; matrix products, arithmetic and copies ran while one was open for 13% of the time, Pallas kernels for 0%

profile of v1, /device:TPU:0, one launch (start us, length us, event | category | flops | bytes accessed | tf_op | source)
XLA Modules:
  0.0 614.6 jit_solution(9866771133390272224)
XLA Ops:
  9.3 5.5 all-to-all-start.1
  17.4 9.7 %all-to-all-done.1 = bf16[192,4,512]{2,0,1:T(8,128)(2,1)S(1)} async-done(((bf16[192,4,512]{2,0,1:T(8,128)(2,1)}), bf16[192,4,512]{2,0,1:T(8,128)(2,1)S(1)}, u32[]{:S(2)}, u32[]{:S(2)}) %all-to-all-start.1) | async-done | bytes 786464 | tf_op jit(solution)/shard_map/all_to_all | solution.py:32
  28.8 3.5 all-to-all-start
  33.3 10.4 %all-to-all-done = bf16[192,4,512]{2,0,1:T(8,128)(2,1)S(1)} async-done(((bf16[192,4,512]{2,0,1:T(8,128)(2,1)}), bf16[192,4,512]{2,0,1:T(8,128)(2,1)S(1)}, u32[]{:S(2)}, u32[]{:S(2)}) %all-to-all-start) | async-done | bytes 786464 | tf_op jit(solution)/shard_map/all_to_all | solution.py:31
  43.6 3.5 all-to-all-start.3
  49.3 8.0 %all-to-all-done.3 = bf16[192,4,512]{2,0,1:T(8,128)(2,1)S(1)} async-done(((bf16[192,4,512]{2,0,1:T(8,128)(2,1)}), bf16[192,4,512]{2,0,1:T(8,128)(2,1)S(1)}, u32[]{:S(2)}, u32[]{:S(2)}) %all-to-all-start.3) | async-done | bytes 786464 | tf_op jit(solution)/shard_map/all_to_all | solution.py:33
  57.3 3.5 all-to-all-start.2
  60.8 9.4 %all-to-all-done.2 = bf16[192,4,512]{2,0,1:T(8,128)(2,1)S(1)} async-done(((bf16[192,4,512]{2,0,1:T(8,128)(2,1)}), bf16[192,4,512]{2,0,1:T(8,128)(2,1)S(1)}, u32[]{:S(2)}, u32[]{:S(2)}) %all-to-all-start.2) | async-done | bytes 786464 | tf_op jit(solution)/shard_map/all_to_all | solution.py:34
  72.7 7.5 %all-to-all-start.4 = ((bf16[32,128,512]{2,1,0:T(8,128)(2,1)}), bf16[32,128,512]{2,1,0:T(8,128)(2,1)}, u32[]{:S(2)}, u32[]{:S(2)}) async-start(bf16[32,128,512]{2,1,0:T(8,128)(2,1)} %stack.3), calls=%async_computation.4 | async-start | bytes 8388608 | tf_op jit(solution)/shard_map/all_to_all | solution.py:18
  81.8 2.8 collective-permute-start
  85.4 2.8 collective-permute-start.1
  94.6 4.9 pad_maximum_fusion
  99.5 5.7 pad_maximum_fusion.1
  105.2 27.7 %all-to-all-done.4 = bf16[32,128,512]{2,1,0:T(8,128)(2,1)} async-done(((bf16[32,128,512]{2,1,0:T(8,128)(2,1)}), bf16[32,128,512]{2,1,0:T(8,128)(2,1)}, u32[]{:S(2)}, u32[]{:S(2)}) %all-to-all-start.4) | async-done | bytes 4194336 | tf_op jit(solution)/shard_map/all_to_all | solution.py:18
  133.0 4.1 gather_fusion.1
  140.7 4.0 gather_fusion
  151.7 219.5 %while.25 = (s32[]{:T(128)}, f32[1152,4,128]{0,2,1:T(8,128)}, f32[1152,4,128]{0,2,1:T(8,128)}, f32[1536,4,128]{0,2,1:T(8,128)}, f32[1536,4,128]{0,2,1:T(8,128)},...) while((s32[]{:T(128)}, f32[1152,4,128]{0,2,1:T(8,128)}, ...), condition=%wide.region_5.6_spmd.clone, body=%wide.region_0.5_spmd.clone.sunk | while | flops 1626605312 | bytes 194795088 | solution.py:158
  161.4 3.4 fusion.55
  179.3 3.6 fusion.57
  197.9 3.4 fusion.55
  215.9 3.6 fusion.57
  234.5 3.4 fusion.55
  252.5 3.5 fusion.57
  271.1 3.4 fusion.55
  289.1 3.6 fusion.57
  307.7 3.4 fusion.55
  325.6 3.5 fusion.57
  344.3 3.4 fusion.55
  362.2 3.5 fusion.57
  371.2 3.2 copy.143
  374.4 2.9 reshape.377
  377.3 4.3 broadcast.238.clone
  381.6 6.1 scatter_fusion
  387.7 6.0 convert_element_type.67
  395.6 2.8 copy.147
  398.4 3.3 reshape.385
  401.7 4.3 broadcast.238.clone.1
  406.1 6.1 scatter_fusion.1
  412.2 5.9 convert_element_type.73
  420.5 4.3 all-to-all-start.6
  441.7 4.7 all-to-all-start.5
  446.6 3.2 collective-permute-done.2
  451.5 39.6 %reduce-scatter.3.cloned.1.call-done = bf16[128,512]{1,0:T(8,128)(2,1)} async-done(((bf16[4096,512]{1,0:T(8,128)(2,1)}), bf16[128,512]{1,0:T(8,128)(2,1)}) %reduce-scatter.3.cloned.1.call-update) | async-done | bytes 131088 | tf_op jit(solution)/shard_map/reduce_scatter | solution.py:182
  491.0 85.3 %reduce-scatter.5.cloned.1.call-done = bf16[128,512]{1,0:T(8,128)(2,1)} async-done(((bf16[4096,512]{1,0:T(8,128)(2,1)}), bf16[128,512]{1,0:T(8,128)(2,1)}) %reduce-scatter.5.cloned.1.call-update) | async-done | bytes 131088 | tf_op jit(solution)/shard_map/reduce_scatter | solution.py:188
  579.1 4.4 all-to-all-start.7
  584.5 9.7 %all-to-all-done.7 = bf16[4,192,512]{2,1,0:T(8,128)(2,1)S(1)} async-done(((bf16[4,192,512]{2,1,0:T(8,128)(2,1)}), bf16[4,192,512]{2,1,0:T(8,128)(2,1)S(1)}, u32[]{:S(2)}, u32[]{:S(2)}) %all-to-all-start.7) | async-done | bytes 786464 | tf_op jit(solution)/shard_map/all_to_all | solution.py:214
  594.2 3.5 all-to-all-start.8
  602.9 4.3 all-to-all-done.8
  (401 shorter events, 234.6 us)
Async XLA Ops:
  7.2 7.7 %copy-start.20 = (s32[192,16]{0,1:T(8,128)S(1)}, s32[192,16]{0,1:T(8,128)}, u32[]{:S(2)}) copy-start(s32[192,16]{0,1:T(8,128)} %param.15) | copy-start | bytes 36868
  7.2 20.7 %copy-start.16 = (bf16[192,2048]{1,0:T(8,128)(2,1)S(1)}, bf16[192,2048]{1,0:T(8,128)(2,1)}, u32[]{:S(2)}) copy-start(bf16[192,2048]{1,0:T(8,128)(2,1)} %param.11) | copy-start | bytes 2359300
  9.3 23.0 %copy-start.17 = (bf16[192,2048]{1,0:T(8,128)(2,1)S(1)}, bf16[192,2048]{1,0:T(8,128)(2,1)}, u32[]{:S(2)}) copy-start(bf16[192,2048]{1,0:T(8,128)(2,1)} %param.13) | copy-start | bytes 2359300
  9.3 17.8 %all-to-all-start.1 = ((bf16[192,4,512]{2,0,1:T(8,128)(2,1)}), bf16[192,4,512]{2,0,1:T(8,128)(2,1)S(1)}, u32[]{:S(2)}, u32[]{:S(2)}) async-start(bf16[192,4,512]{2,0,1:T(8,128)(2,1)} %bitcast.109), calls=%async_computation.1 | async-start | bytes 1572864 | tf_op jit(solution)/shard_map/all_to_all | solution.py:32
  14.9 125.9 %all-gather.3.cloned.1.call-start = ((), (), s32[]{:S(2)}) async-start(), calls=%async_computation.13 | async-start | bytes 4325376 | tf_op jit(solution)/shard_map/all_gather | solution.py:59
  28.8 14.8 %all-to-all-start = ((bf16[192,4,512]{2,0,1:T(8,128)(2,1)}), bf16[192,4,512]{2,0,1:T(8,128)(2,1)S(1)}, u32[]{:S(2)}, u32[]{:S(2)}) async-start(bf16[192,4,512]{2,0,1:T(8,128)(2,1)} %bitcast.110), calls=%async_computation | async-start | bytes 1572864 | tf_op jit(solution)/shard_map/all_to_all | solution.py:31
  43.6 13.6 %all-to-all-start.3 = ((bf16[192,4,512]{2,0,1:T(8,128)(2,1)}), bf16[192,4,512]{2,0,1:T(8,128)(2,1)S(1)}, u32[]{:S(2)}, u32[]{:S(2)}) async-start(bf16[192,4,512]{2,0,1:T(8,128)(2,1)} %bitcast.107), calls=%async_computation.3 | async-start | bytes 1572864 | tf_op jit(solution)/shard_map/all_to_all | solution.py:33
  57.3 13.0 %all-to-all-start.2 = ((bf16[192,4,512]{2,0,1:T(8,128)(2,1)}), bf16[192,4,512]{2,0,1:T(8,128)(2,1)S(1)}, u32[]{:S(2)}, u32[]{:S(2)}) async-start(bf16[192,4,512]{2,0,1:T(8,128)(2,1)} %bitcast.175), calls=%async_computation.2 | async-start | bytes 1572864 | tf_op jit(solution)/shard_map/all_to_all | solution.py:34
  72.7 60.2 %all-to-all-start.4 = ((bf16[32,128,512]{2,1,0:T(8,128)(2,1)}), bf16[32,128,512]{2,1,0:T(8,128)(2,1)}, u32[]{:S(2)}, u32[]{:S(2)}) async-start(bf16[32,128,512]{2,1,0:T(8,128)(2,1)} %stack.3), calls=%async_computation.4 | async-start | bytes 8388608 | tf_op jit(solution)/shard_map/all_to_all | solution.py:18
  80.2 410.8 %reduce-scatter.3.cloned.1.call-start = ((), (), s32[]{:S(2)}) async-start(), calls=%async_computation.11 | async-start | bytes 4325376 | tf_op jit(solution)/shard_map/reduce_scatter | solution.py:182
  81.8 10.7 %collective-permute-start = (bf16[384,512]{1,0:T(8,128)(2,1)}, bf16[384,512]{1,0:T(8,128)(2,1)}, u32[]{:S(2)}, u32[]{:S(2)}) collective-permute-start(bf16[384,512]{1,0:T(8,128)(2,1)} %bitcast.2), channel_id=1, source_target_pairs={{0,4},{4,8},{8,12},{12,16},{16,20},{20,24},{24,28},{28,32},{32,36}... | collective-permute-start | bytes 1179656 | tf_op jit(solution)/shard_map/ppermute | solution.py:26
  85.4 8.7 %collective-permute-start.1 = (bf16[384,512]{1,0:T(8,128)(2,1)}, bf16[384,512]{1,0:T(8,128)(2,1)S(1)}, u32[]{:S(2)}, u32[]{:S(2)}) collective-permute-start(bf16[384,512]{1,0:T(8,128)(2,1)} %bitcast.13), channel_id=1, source_target_pairs={{0,4},{4,8},{8,12},{12,16},{16,20},{20,24},{24,28},{28,32},{32,36}... | collective-permute-start | bytes 1179656 | tf_op jit(solution)/shard_map/ppermute | solution.py:26
  93.9 5.6 copy-start.14
  151.7 5.9 copy-start.12
  153.0 4.9 copy-start.10
  158.1 6.7 %copy-start.7 = (bf16[2048,4,128]{2,0,1:T(8,128)(2,1)}, bf16[2048,4,128]{2,0,1:T(8,128)(2,1)S(1)}, u32[]{:S(2)}) copy-start(bf16[2048,4,128]{2,0,1:T(8,128)(2,1)S(1)} %constant_dynamic-update-slice_fusion.5) | copy-start | bytes 6291460 | tf_op jit(solution)/shard_map/while
  179.3 4.2 copy-start.4
  183.5 4.8 copy-start.13
  188.3 5.9 copy-start.12
  189.6 4.9 copy-start.10
  194.7 6.7 %copy-start.7 = (bf16[2048,4,128]{2,0,1:T(8,128)(2,1)}, bf16[2048,4,128]{2,0,1:T(8,128)(2,1)S(1)}, u32[]{:S(2)}) copy-start(bf16[2048,4,128]{2,0,1:T(8,128)(2,1)S(1)} %constant_dynamic-update-slice_fusion.5) | copy-start | bytes 6291460 | tf_op jit(solution)/shard_map/while
  220.1 4.8 copy-start.13
  224.8 5.9 copy-start.12
  226.2 4.9 copy-start.10
  231.3 6.7 %copy-start.7 = (bf16[2048,4,128]{2,0,1:T(8,128)(2,1)}, bf16[2048,4,128]{2,0,1:T(8,128)(2,1)S(1)}, u32[]{:S(2)}) copy-start(bf16[2048,4,128]{2,0,1:T(8,128)(2,1)S(1)} %constant_dynamic-update-slice_fusion.5) | copy-start | bytes 6291460 | tf_op jit(solution)/shard_map/while
  252.5 4.2 copy-start.4
  256.6 4.8 copy-start.13
  261.4 5.9 copy-start.12
  262.7 4.9 copy-start.10
  267.9 6.7 %copy-start.7 = (bf16[2048,4,128]{2,0,1:T(8,128)(2,1)}, bf16[2048,4,128]{2,0,1:T(8,128)(2,1)S(1)}, u32[]{:S(2)}) copy-start(bf16[2048,4,128]{2,0,1:T(8,128)(2,1)S(1)} %constant_dynamic-update-slice_fusion.5) | copy-start | bytes 6291460 | tf_op jit(solution)/shard_map/while
  293.2 4.8 copy-start.13
  298.0 5.9 copy-start.12
  299.3 4.9 copy-start.10
  304.4 6.7 %copy-start.7 = (bf16[2048,4,128]{2,0,1:T(8,128)(2,1)}, bf16[2048,4,128]{2,0,1:T(8,128)(2,1)S(1)}, u32[]{:S(2)}) copy-start(bf16[2048,4,128]{2,0,1:T(8,128)(2,1)S(1)} %constant_dynamic-update-slice_fusion.5) | copy-start | bytes 6291460 | tf_op jit(solution)/shard_map/while
  329.8 4.8 copy-start.13
  334.6 5.9 copy-start.12
  335.9 4.9 copy-start.10
  341.0 6.7 %copy-start.7 = (bf16[2048,4,128]{2,0,1:T(8,128)(2,1)}, bf16[2048,4,128]{2,0,1:T(8,128)(2,1)S(1)}, u32[]{:S(2)}) copy-start(bf16[2048,4,128]{2,0,1:T(8,128)(2,1)S(1)} %constant_dynamic-update-slice_fusion.5) | copy-start | bytes 6291460 | tf_op jit(solution)/shard_map/while
  366.4 4.8 copy-start.13
  377.3 4.3 copy-start.11
  393.8 182.5 %reduce-scatter.5.cloned.1.call-start = ((), (), s32[]{:S(2)}) async-start(), calls=%async_computation.12 | async-start | bytes 4325376 | tf_op jit(solution)/shard_map/reduce_scatter | solution.py:188
  420.5 11.2 %copy-start.21 = (s32[3]{0:T(128)S(1)}, s32[3]{0:T(128)}, u32[]{:S(2)}) copy-start(s32[3]{0:T(128)} %constant.137.clone.1) | copy-start | bytes 40
  420.5 21.2 %all-to-all-start.6 = ((bf16[4,192,512]{2,1,0:T(8,128)(2,1)}), bf16[4,192,512]{2,1,0:T(8,128)(2,1)}, u32[]{:S(2)}, u32[]{:S(2)}) async-start(bf16[4,192,512]{2,1,0:T(8,128)(2,1)} %all_to_all.120), calls=%async_computation.6 | async-start | bytes 1572864 | tf_op jit(solution)/shard_map/all_to_all | solution.py:213
  427.0 19.4 %collective-permute-start.3 = (bf16[384,512]{1,0:T(8,128)(2,1)}, bf16[384,512]{1,0:T(8,128)(2,1)S(1)}, u32[]{:S(2)}, u32[]{:S(2)}) collective-permute-start(bf16[384,512]{1,0:T(8,128)(2,1)} %copy.157), channel_id=1, source_target_pairs={{4,0},{8,4},{12,8},{16,12},{20,16},{24,20},{28,24},{32,28},{36,32}... | collective-permute-start | bytes 1179656 | tf_op jit(solution)/shard_map/ppermute | solution.py:26
  430.4 19.4 %collective-permute-start.2 = (bf16[384,512]{1,0:T(8,128)(2,1)}, bf16[384,512]{1,0:T(8,128)(2,1)}, u32[]{:S(2)}, u32[]{:S(2)}) collective-permute-start(bf16[384,512]{1,0:T(8,128)(2,1)} %copy.155), channel_id=1, source_target_pairs={{4,0},{8,4},{12,8},{16,12},{20,16},{24,20},{28,24},{32,28},{36,32}... | collective-permute-start | bytes 1179656 | tf_op jit(solution)/shard_map/ppermute | solution.py:26
  441.7 137.4 %all-to-all-start.5 = ((bf16[4,192,512]{2,1,0:T(8,128)(2,1)}), bf16[4,192,512]{2,1,0:T(8,128)(2,1)}, u32[]{:S(2)}, u32[]{:S(2)}) async-start(bf16[4,192,512]{2,1,0:T(8,128)(2,1)} %all_to_all.116), calls=%async_computation.5 | async-start | bytes 1572864 | tf_op jit(solution)/shard_map/all_to_all | solution.py:212
  579.1 15.1 %all-to-all-start.7 = ((bf16[4,192,512]{2,1,0:T(8,128)(2,1)}), bf16[4,192,512]{2,1,0:T(8,128)(2,1)S(1)}, u32[]{:S(2)}, u32[]{:S(2)}) async-start(bf16[4,192,512]{2,1,0:T(8,128)(2,1)} %bitcast.176), calls=%async_computation.8 | async-start | bytes 1572864 | tf_op jit(solution)/shard_map/all_to_all | solution.py:214
  594.2 13.0 %all-to-all-start.8 = ((bf16[4,192,512]{2,1,0:T(8,128)(2,1)}), bf16[4,192,512]{2,1,0:T(8,128)(2,1)S(1)}, u32[]{:S(2)}, u32[]{:S(2)}) async-start(bf16[4,192,512]{2,1,0:T(8,128)(2,1)} %bitcast.31), calls=%async_computation.10 | async-start | bytes 1572864 | tf_op jit(solution)/shard_map/all_to_all | solution.py:215
  (50 other events, 131.4 us)
Sparse Core Ops, SparseCore 0:
  28.0 45.4 all-gather.2
  393.9 97.0 reduce-scatter.2
  495.1 81.1 reduce-scatter.4
